TPU v7x, 32 devices: a whole 2x2x4 slice. The times are simulated.
32 devices in a mesh: seq: 8 (over z, x), doc: 4 (over y, core).
Axes of the slice: x: 2, y: 2, z: 4, core: 2. Of those that a mesh axis runs over, the one named last changes fastest.
Arguments:
- queries: bfloat16 [4096, 2048], P(('doc', 'seq')), parts along dimension 0, may hold values from -5 to 5
- key_rows: bfloat16 [4096, 2048], P(('doc', 'seq')), parts along dimension 0, may hold values from -5 to 5
- value_rows: bfloat16 [4096, 2048], P(('doc', 'seq')), parts along dimension 0, may hold values from -6 to 6
- out_grad: bfloat16 [4096, 2048], P(('doc', 'seq')), parts along dimension 0, may hold values from -6 to 6
- vertical: int32 [64, 6], P('doc'), parts along dimension 0, may hold values from 0 to 7, as said below
- slash_offsets: int32 [64, 6], P('doc'), parts along dimension 0, may hold values from -7 to 7, as said below
- counts: int32 [64, 2], P('doc'), parts along dimension 0, may hold values from 1 to 6, as said below
Outputs:
- query_grad: bfloat16 [4096, 2048], P(('doc', 'seq')), parts along dimension 0
- key_grad: bfloat16 [4096, 2048], P(('doc', 'seq')), parts along dimension 0
- value_grad: bfloat16 [4096, 2048], P(('doc', 'seq')), parts along dimension 0
There are 4 independent parts, one for each index of `doc`. A program takes and returns all parts, laid end to end along the dimension named above; each array names one. Nothing has to cross between parts.
Inputs may be any that keep to these rules, and one draw needn't show every extreme that they name: counts[h, 0] is 1 to 6 and counts[h, 1] is 1 to 6; some head has both at their most and some head both at 1. `vertical`: the entries of a head are distinct. `slash_offsets`: the entries of a head are distinct and slash_offsets[h, 0] is 0 for every head.
All inputs are finite; a program needn't handle non-finite values.
Results may differ from a plain program's by a relative error of at most 0.0086.
Values may be sent and summed in bfloat16 or wider, within the bound.
A program may use at most 64 MiB of HBM per device.

v0:
```python
import functools

import jax
import jax.numpy as jnp
from jax import lax
from jax.experimental import pallas as pl
from jax.experimental.pallas import tpu as pltpu
from jax.sharding import PartitionSpec as P

HEADS = 16
HEAD_DIM = 128
BLK = 128


block_group = 4


def block_lists(chosen, vert_head, slash_head, count_head, nblocks):
    vert_cap = vert_head.shape[0]
    slash_cap = slash_head.shape[0]
    rows_now = chosen.shape[0]
    vert_index = jnp.broadcast_to(vert_head[None, :], (rows_now, vert_cap))
    vert_valid = jnp.broadcast_to(
        (jnp.arange(vert_cap, dtype=jnp.int32) < count_head[0])[None, :], (rows_now, vert_cap)
    )
    slash_index = chosen[:, None] - slash_head[None, :]
    inside = (slash_index >= 0) & (slash_index < nblocks)
    repeated = jnp.any(
        (vert_index[:, :, None] == slash_index[:, None, :]) & vert_valid[:, :, None], axis=1
    )
    slash_valid = (
        (jnp.arange(slash_cap, dtype=jnp.int32) < count_head[1])[None, :]
        & inside
        & jnp.logical_not(repeated)
    )
    index_table = jnp.clip(jnp.concatenate([vert_index, slash_index], axis=1), 0, nblocks - 1)
    valid_table = jnp.concatenate([vert_valid, slash_valid], axis=1)
    return (index_table, valid_table)


def owner_backward(
    q_blocks, k_blocks, v_blocks, d_blocks, vert_head, slash_head, count_head, chosen_all
):
    nblocks, blk_rows, head_dim = q_blocks.shape
    score_scale = head_dim ** (-0.5)
    vert_cap = vert_head.shape[0]
    trips = count_head[0] + count_head[1]

    def one_group(carried, chosen):
        key_acc, value_acc = carried
        index_table, valid_table = block_lists(chosen, vert_head, slash_head, count_head, nblocks)
        q_group = q_blocks[chosen]
        d_group = d_blocks[chosen]
        group_shape = (chosen.shape[0], blk_rows, 1)

        def fetch(position):
            slot_pick = jnp.where(
                position < count_head[0], position, vert_cap + position - count_head[0]
            )
            column = lax.dynamic_index_in_dim(index_table, slot_pick, 1, keepdims=False)
            usable = lax.dynamic_index_in_dim(valid_table, slot_pick, 1, keepdims=False)[
                :, None, None
            ]
            k_tile = k_blocks[column]
            v_tile = v_blocks[column]
            scores = (
                jnp.einsum("gqd,gkd->gqk", q_group, k_tile, preferred_element_type=jnp.float32)
                * score_scale
            )
            return (column, usable, k_tile, v_tile, scores)

        def row_stats(position, running):
            row_top, row_total = running
            column, usable, k_tile, v_tile, scores = fetch(position)
            new_top = jnp.maximum(
                row_top, jnp.where(usable, jnp.max(scores, axis=-1, keepdims=True), -1e30)
            )
            added = jnp.where(
                usable, jnp.sum(jnp.exp(scores - new_top), axis=-1, keepdims=True), 0.0
            )
            return (new_top, row_total * jnp.exp(row_top - new_top) + added)

        row_top, row_total = lax.fori_loop(
            0,
            trips,
            row_stats,
            (jnp.full(group_shape, -1e30, jnp.float32), jnp.zeros(group_shape, jnp.float32)),
        )

        def probs_of(scores, usable):
            return jnp.where(usable, jnp.exp(scores - row_top) / row_total, 0.0)

        def output_step(position, running):
            column, usable, k_tile, v_tile, scores = fetch(position)
            weights = probs_of(scores, usable).astype(jnp.bfloat16)
            return running + jnp.einsum(
                "gqk,gkd->gqd", weights, v_tile, preferred_element_type=jnp.float32
            )

        attended = lax.fori_loop(
            0, trips, output_step, jnp.zeros((chosen.shape[0], blk_rows, head_dim), jnp.float32)
        )
        row_delta = jnp.sum(d_group.astype(jnp.float32) * attended, axis=-1, keepdims=True)

        def grad_step(position, running):
            query_acc, key_run, value_run = running
            column, usable, k_tile, v_tile, scores = fetch(position)
            probs = probs_of(scores, usable)
            weights = probs.astype(jnp.bfloat16)
            grad_probs = jnp.einsum(
                "gqd,gkd->gqk", d_group, v_tile, preferred_element_type=jnp.float32
            )
            grad_scores = (probs * (grad_probs - row_delta)).astype(jnp.bfloat16)
            query_acc = query_acc + jnp.einsum(
                "gqk,gkd->gqd", grad_scores, k_tile, preferred_element_type=jnp.float32
            )
            key_part = (
                jnp.einsum("gqk,gqd->gkd", grad_scores, q_group, preferred_element_type=jnp.float32)
                * score_scale
            )
            value_part = jnp.einsum(
                "gqk,gqd->gkd", weights, d_group, preferred_element_type=jnp.float32
            )
            return (
                query_acc,
                key_run.at[column].add(key_part),
                value_run.at[column].add(value_part),
            )

        start_query = jnp.zeros((chosen.shape[0], blk_rows, head_dim), jnp.float32)
        query_acc, key_acc, value_acc = lax.fori_loop(
            0, trips, grad_step, (start_query, key_acc, value_acc)
        )
        return ((key_acc, value_acc), query_acc * score_scale)

    zeros_acc = jnp.zeros((nblocks, blk_rows, head_dim), jnp.float32)
    (key_acc, value_acc), query_grad = lax.scan(one_group, (zeros_acc, zeros_acc), chosen_all)
    return (query_grad.reshape(-1, blk_rows, head_dim), key_acc, value_acc)


def split_head_body(queries, key_rows, value_rows, out_grad, vertical, slash_offsets, counts):
    tokens_here = queries.shape[0]
    device_count = lax.axis_size("seq")
    device_here = lax.axis_index("seq")
    full_width = HEADS * HEAD_DIM

    def doubled(matrix):
        return jnp.repeat(matrix.reshape(tokens_here, HEADS, HEAD_DIM), 2, axis=1)

    q_owned, k_owned, v_owned, d_owned = (
        lax.all_to_all(doubled(queries), "seq", split_axis=1, concat_axis=0, tiled=True),
        lax.all_to_all(doubled(key_rows), "seq", split_axis=1, concat_axis=0, tiled=True),
        lax.all_to_all(doubled(value_rows), "seq", split_axis=1, concat_axis=0, tiled=True),
        lax.all_to_all(doubled(out_grad), "seq", split_axis=1, concat_axis=0, tiled=True),
    )
    length = tokens_here * device_count
    nblocks = length // BLK
    per_device = 2 * HEADS // device_count
    query_parts = []
    key_parts = []
    value_parts = []
    for local_slot in range(per_device):
        slot_index = device_here * per_device + local_slot
        head_index = slot_index // 2
        parity = slot_index % 2
        chosen_all = (parity + 2 * jnp.arange(nblocks // 2, dtype=jnp.int32)).reshape(
            -1, block_group
        )

        def blockwise(matrix):
            return matrix[:, local_slot, :].reshape(nblocks, BLK, HEAD_DIM)

        query_sel, key_acc, value_acc = owner_backward(
            blockwise(q_owned),
            blockwise(k_owned),
            blockwise(v_owned),
            blockwise(d_owned),
            vertical[head_index],
            slash_offsets[head_index],
            counts[head_index],
            chosen_all,
        )
        query_full = (
            jnp.zeros((nblocks, BLK, HEAD_DIM), jnp.float32)
            .at[chosen_all.reshape(-1)]
            .set(query_sel)
        )
        query_parts.append(query_full.reshape(length, HEAD_DIM))
        key_parts.append(key_acc.reshape(length, HEAD_DIM))
        value_parts.append(value_acc.reshape(length, HEAD_DIM))
    all_parts = (query_parts, key_parts, value_parts)
    stacked = [jnp.stack(member, axis=1) for member in all_parts]
    returned = (
        lax.all_to_all(stacked[0], "seq", split_axis=0, concat_axis=1, tiled=True),
        lax.all_to_all(stacked[1], "seq", split_axis=0, concat_axis=1, tiled=True),
        lax.all_to_all(stacked[2], "seq", split_axis=0, concat_axis=1, tiled=True),
    )
    results = [
        back.reshape(tokens_here, HEADS, 2, HEAD_DIM)
        .sum(axis=2)
        .astype(jnp.bfloat16)
        .reshape(tokens_here, full_width)
        for back in returned
    ]
    return (results[0], results[1], results[2])


MESH = pl.DeviceIdType.MESH
QUERY_TILE = 256
LOG2E = 1.4426950408889634
NEVER = -1e30


def fused_kernel(
    count,
    per_device,
    k_in,
    v_in,
    q_in,
    d_in,
    vertical,
    slash_offsets,
    counts,
    dq_out,
    dk_out,
    dv_out,
    arrived,
    finished,
    bias,
    key_acc,
    value_acc,
    fwd_send,
    fwd_recv,
    fwd_local,
    back_send,
    back_recv,
    back_local,
):
    me = lax.axis_index("seq")
    sources = (k_in, v_in, q_in, d_in)
    targets = (dk_out, dv_out, dq_out)
    length = count * BLK
    score_scale = HEAD_DIM ** (-0.5)

    def offset_of(step):
        return count // 2 + ((step + 1) // 2) * (2 * (step % 2) - 1)

    def rows_of(index):
        return pl.ds(pl.multiple_of(index * BLK, BLK), BLK)

    def columns_of(owner, slot):
        return pl.ds(pl.multiple_of((owner * per_device + slot) * HEAD_DIM, HEAD_DIM), HEAD_DIM)

    def forward(which, slot, step, sending):
        peer = lax.rem(me + offset_of(step), count)
        source = lax.rem(me + count - offset_of(step), count)
        return pltpu.make_async_remote_copy(
            src_ref=sources[which].at[:, columns_of(peer, slot)],
            dst_ref=arrived.at[which, slot, rows_of(me if sending else source), :],
            send_sem=fwd_send.at[which, slot, step],
            recv_sem=fwd_recv.at[which, slot, step],
            device_id={"seq": peer},
            device_id_type=MESH,
        )

    def own_forward(which, slot):
        return pltpu.make_async_copy(
            sources[which].at[:, columns_of(me, slot)],
            arrived.at[which, slot, rows_of(me), :],
            fwd_local.at[which, slot],
        )

    def backward(which, slot, step, sending):
        peer = lax.rem(me + offset_of(step), count)
        source = lax.rem(me + count - offset_of(step), count)
        return pltpu.make_async_remote_copy(
            src_ref=finished.at[which, slot, rows_of(peer), :],
            dst_ref=targets[which].at[:, columns_of(me if sending else source, slot)],
            send_sem=back_send.at[which, slot, step],
            recv_sem=back_recv.at[which, slot, step],
            device_id={"seq": peer},
            device_id_type=MESH,
        )

    def own_backward(which, slot):
        return pltpu.make_async_copy(
            finished.at[which, slot, rows_of(me), :],
            targets[which].at[:, columns_of(me, slot)],
            back_local.at[which, slot],
        )

    def each_step(do):
        @pl.loop(0, count - 1)
        def _(step):
            do(step)

    barrier = pltpu.get_barrier_semaphore()

    @pl.loop(1, count)
    def _(step):
        pl.semaphore_signal(
            barrier, inc=1, device_id={"seq": lax.rem(me + step, count)}, device_id_type=MESH
        )

    pl.semaphore_wait(barrier, count - 1)

    for slot in range(per_device):

        def send_all(step, slot=slot):
            for which in range(4):
                forward(which, slot, step, True).start()

        each_step(send_all)
        for which in range(4):
            own_forward(which, slot).start()

    query_block = lax.broadcasted_iota(jnp.int32, (count, length), 0)
    key_block = lax.broadcasted_iota(jnp.int32, (count, length), 1) // BLK
    for slot in range(per_device):
        head = me * per_device + slot
        allowed = jnp.zeros((count, length), jnp.float32)
        for entry in range(vertical.shape[0]):
            wanted = jnp.where(entry < counts[0, head], vertical[entry, head], -1)
            allowed = jnp.where(key_block == wanted, 1.0, allowed)
        for entry in range(slash_offsets.shape[0]):
            wanted = jnp.where(entry < counts[1, head], slash_offsets[entry, head], 2 * count)
            allowed = jnp.where(query_block - key_block == wanted, 1.0, allowed)
        bias[slot] = jnp.where(allowed > 0.0, 0.0, NEVER)

    def dot(a, b, a_dim, b_dim):
        return lax.dot_general(
            a, b, (((a_dim,), (b_dim,)), ((), ())), preferred_element_type=jnp.float32
        )

    for slot in range(per_device):

        def arrive(step, slot=slot):
            for which in range(4):
                forward(which, slot, step, False).wait_recv()

        each_step(arrive)
        for which in range(4):
            own_forward(which, slot).wait()

        key_acc[...] = jnp.zeros_like(key_acc)
        value_acc[...] = jnp.zeros_like(value_acc)

        @pl.loop(0, length // QUERY_TILE)
        def _(tile, slot=slot):
            rows = pl.ds(pl.multiple_of(tile * QUERY_TILE, QUERY_TILE), QUERY_TILE)
            keys = arrived[0, slot]
            values = arrived[1, slot]
            q_tile = arrived[2, slot, rows, :]
            d_tile = arrived[3, slot, rows, :]
            blocks_here = QUERY_TILE // BLK
            mask = jnp.concatenate(
                [
                    jnp.broadcast_to(
                        bias[slot, pl.ds(tile * blocks_here + part, 1), :], (BLK, length)
                    )
                    for part in range(blocks_here)
                ],
                axis=0,
            )
            scores = dot(q_tile, keys, 1, 1) * (score_scale * LOG2E) + mask
            top = jnp.max(scores, axis=-1, keepdims=True)
            raised = jnp.exp2(scores - top)
            total = jnp.sum(raised, axis=-1, keepdims=True)
            probs = raised * (1.0 / total)
            weights = probs.astype(jnp.bfloat16)
            attended = dot(weights, values, 1, 0)
            row_delta = jnp.sum(d_tile.astype(jnp.float32) * attended, axis=-1, keepdims=True)
            grad_probs = dot(d_tile, values, 1, 1)
            grad_scores = (probs * (grad_probs - row_delta)).astype(jnp.bfloat16)
            finished[2, slot, rows, :] = (dot(grad_scores, keys, 1, 0) * score_scale).astype(
                jnp.bfloat16
            )
            key_acc[...] += dot(q_tile, grad_scores, 0, 0)
            value_acc[...] += dot(d_tile, weights, 0, 0)

        finished[0, slot] = (key_acc[...] * score_scale).T.astype(jnp.bfloat16)
        finished[1, slot] = value_acc[...].T.astype(jnp.bfloat16)

        def give_back(step, slot=slot):
            for which in range(3):
                backward(which, slot, step, True).start()

        each_step(give_back)
        for which in range(3):
            own_backward(which, slot).start()

    for slot in range(per_device):

        def drain(step, slot=slot):
            for which in range(4):
                forward(which, slot, step, True).wait_send()
            for which in range(3):
                backward(which, slot, step, True).wait_send()
                backward(which, slot, step, False).wait_recv()

        each_step(drain)
        for which in range(3):
            own_backward(which, slot).wait()


def store_kernel(dq_in, dk_in, dv_in, dq_out, dk_out, dv_out, held, load_sem, store_sem):
    sources = (dq_in, dk_in, dv_in)
    targets = (dq_out, dk_out, dv_out)
    loads = [
        pltpu.make_async_copy(src, held.at[i], load_sem.at[i]) for i, src in enumerate(sources)
    ]
    stores = [
        pltpu.make_async_copy(held.at[i], dst, store_sem.at[i]) for i, dst in enumerate(targets)
    ]
    for load in loads:
        load.start()
    for load, store in zip(loads, stores):
        load.wait()
        store.start()
    for store in stores:
        store.wait()


def whole_head_body(queries, key_rows, value_rows, out_grad, vertical, slash_offsets, counts):
    count = lax.axis_size("seq")
    per_device = HEADS // count
    length = count * BLK
    anywhere = pl.BlockSpec(memory_space=pl.ANY)
    scalars = pl.BlockSpec(memory_space=pltpu.SMEM)
    shape = jax.ShapeDtypeStruct(queries.shape, queries.dtype)
    sems = pltpu.SemaphoreType.DMA
    query_grad, key_grad, value_grad = pl.pallas_call(
        functools.partial(fused_kernel, count, per_device),
        out_shape=(shape, shape, shape),
        in_specs=[anywhere] * 4 + [scalars] * 3,
        out_specs=(anywhere, anywhere, anywhere),
        scratch_shapes=[
            pltpu.VMEM((4, per_device, length, HEAD_DIM), jnp.bfloat16),
            pltpu.VMEM((3, per_device, length, HEAD_DIM), jnp.bfloat16),
            pltpu.VMEM((per_device, count, length), jnp.float32),
            pltpu.VMEM((HEAD_DIM, length), jnp.float32),
            pltpu.VMEM((HEAD_DIM, length), jnp.float32),
            sems((4, per_device, count - 1)),
            sems((4, per_device, count - 1)),
            sems((4, per_device)),
            sems((3, per_device, count - 1)),
            sems((3, per_device, count - 1)),
            sems((3, per_device)),
        ],
        compiler_params=pltpu.CompilerParams(
            collective_id=0, has_side_effects=True, vmem_limit_bytes=64 * 1024 * 1024
        ),
    )(key_rows, value_rows, queries, out_grad, vertical.T, slash_offsets.T, counts.T)
    return pl.pallas_call(
        store_kernel,
        out_shape=(shape, shape, shape),
        in_specs=[anywhere] * 3,
        out_specs=(anywhere,) * 3,
        scratch_shapes=[pltpu.VMEM((3, *shape.shape), shape.dtype), sems((3,)), sems((3,))],
        compiler_params=pltpu.CompilerParams(vmem_limit_bytes=64 * 1024 * 1024),
    )(query_grad, key_grad, value_grad)


def solution(mesh):
    whole_heads = HEADS % mesh.shape["seq"] == 0
    return jax.shard_map(
        whole_head_body if whole_heads else split_head_body,
        mesh=mesh,
        in_specs=(
            P(("doc", "seq"), None),
            P(("doc", "seq"), None),
            P(("doc", "seq"), None),
            P(("doc", "seq"), None),
            P("doc", None),
            P("doc", None),
            P("doc", None),
        ),
        out_specs=(P(("doc", "seq"), None), P(("doc", "seq"), None), P(("doc", "seq"), None)),
        check_vma=False,
    )
```

profile of v0, /device:TPU:0, one launch (start us, length us, event | category | flops | bytes accessed | tf_op | source)
XLA Modules:
  0.0 89.8 jit_solution(5854237192878987097)
XLA Ops:
  0.6 87.0 %shard_map.94 = (bf16[128,2048]{1,0:T(8,128)(2,1)}, bf16[128,2048]{1,0:T(8,128)(2,1)}, bf16[128,2048]{1,0:T(8,128)(2,1)}) custom-call(bf16[128,2048]{1,0:T(8,128)(2,1)} %k_in.1, bf16[128,2048]{1,0:T(8,128)(2,1)} %v_in.1, bf16[128,2048]{1,0:T(8,128)(2,1)} %q_in.1, bf16[128,2048]{1,0:T(8,128)(2,1)} %d_in.1, s32[6,16]{1,0:T(8,128)} %bitcast.3, ...), custom_call_target="tpu_custom_call" | custom-call | tf_op jit(solution)/shard_map/pallas_call | solution.py:432
  87.6 2.2 %shard_map.95 = (bf16[128,2048]{1,0:T(8,128)(2,1)}, bf16[128,2048]{1,0:T(8,128)(2,1)}, bf16[128,2048]{1,0:T(8,128)(2,1)}) custom-call(bf16[128,2048]{1,0:T(8,128)(2,1)} %get-tuple-element.6.dq_in, bf16[128,2048]{1,0:T(8,128)(2,1)} %get-tuple-element.7.dk_in, bf16[128,2048]{1,0:T(8,128)(2,1)} %get-tuple-element.8.dv_in), custom_call_target="tpu_custom_call" | custom-call | tf_op jit(solution)/shard_map/pallas_call | solution.py:454
where the time goes:
time: 90 us; the launch traced here: 89.8 us
  Pallas kernels  89.2 us (99%)
    pallas_call x1, Pallas kernels, whole_head_body(): pl.pallas_call(functools.partial(fused_kernel, count, per_device), out_sh...  87 us
    pallas_call x1, Pallas kernels, whole_head_body(): pl.pallas_call(store_kernel, out_shape=(shape, shape, shape), in_specs=[a...  2.23 us

commit v1 on v0

--- a/solution.py
+++ b/solution.py
@@ -206,7 +206,7 @@
 
 
 MESH = pl.DeviceIdType.MESH
-QUERY_TILE = 256
+QUERY_TILE = 512
 LOG2E = 1.4426950408889634
 NEVER = -1e30
 

time: 90 us -> 90 us (level)
  no operation moved by 1% of the time
where the time goes in v1:
time: 90 us; the launch traced here: 89.8 us
  Pallas kernels  89.2 us (99%)
    pallas_call x1, Pallas kernels, whole_head_body(): pl.pallas_call(functools.partial(fused_kernel, count, per_device), out_sh...  87 us
    pallas_call x1, Pallas kernels, whole_head_body(): pl.pallas_call(store_kernel, out_shape=(shape, shape, shape), in_specs=[a...  2.23 us

profile of v1, /device:TPU:0, one launch (start us, length us, event | category | flops | bytes accessed | tf_op | source)
XLA Modules:
  0.0 89.8 jit_solution(9479666775609485353)
XLA Ops:
  0.6 87.0 %shard_map.94 = (bf16[128,2048]{1,0:T(8,128)(2,1)}, bf16[128,2048]{1,0:T(8,128)(2,1)}, bf16[128,2048]{1,0:T(8,128)(2,1)}) custom-call(bf16[128,2048]{1,0:T(8,128)(2,1)} %k_in.1, bf16[128,2048]{1,0:T(8,128)(2,1)} %v_in.1, bf16[128,2048]{1,0:T(8,128)(2,1)} %q_in.1, bf16[128,2048]{1,0:T(8,128)(2,1)} %d_in.1, s32[6,16]{1,0:T(8,128)} %bitcast.3, ...), custom_call_target="tpu_custom_call" | custom-call | tf_op jit(solution)/shard_map/pallas_call | solution.py:432
  87.6 2.2 %shard_map.95 = (bf16[128,2048]{1,0:T(8,128)(2,1)}, bf16[128,2048]{1,0:T(8,128)(2,1)}, bf16[128,2048]{1,0:T(8,128)(2,1)}) custom-call(bf16[128,2048]{1,0:T(8,128)(2,1)} %get-tuple-element.6.dq_in, bf16[128,2048]{1,0:T(8,128)(2,1)} %get-tuple-element.7.dk_in, bf16[128,2048]{1,0:T(8,128)(2,1)} %get-tuple-element.8.dv_in), custom_call_target="tpu_custom_call" | custom-call | tf_op jit(solution)/shard_map/pallas_call | solution.py:454
